TPU v7x, 128 devices: a whole 4x4x4 slice. The times are simulated.
128 devices in a mesh: dp: 16 (over y_hi, x, core), space: 8 (over z, y_lo).
Axes of the slice: x: 4, y: 4 (y_hi: 2, y_lo: 2; y = y_hi * 2 + y_lo), z: 4, core: 2. Of those that a mesh axis runs over, the one named last changes fastest.
Arguments:
- volume: bfloat16 [16, 32, 32, 128], P('dp', 'space'), may hold values from -6 to 6
- first_kernel: bfloat16 [3, 3, 3, 4, 64], replicated, may hold values from -0.625 to 0.625
- mid_kernel: bfloat16 [3, 3, 3, 64, 128], replicated, may hold values from -0.15625 to 0.15625
- deep_kernel: bfloat16 [3, 3, 3, 128, 256], replicated, may hold values from -0.109375 to 0.109375
- deep_cotangent: bfloat16 [16, 16, 16, 16, 256], P('dp', 'space'), may hold values from -6 to 6
Outputs:
- deep_output: bfloat16 [16, 16, 16, 16, 256], P('dp', 'space')
- deep_kernel_grad: float32 [3, 3, 3, 128, 256], P(None, None, None, 'space')
- mid_kernel_grad: float32 [3, 3, 3, 64, 128], replicated
All inputs are finite; a program needn't handle non-finite values.
Results may differ from a plain program's by a relative error of at most 0.024.
Values may be sent and summed in bfloat16 or wider, within the bound.
A program may use at most 128 MiB of HBM per device.

v0:
```python
import math
import jax
import jax.numpy as jnp
from jax import lax
from jax.sharding import PartitionSpec as P

SLOPE = 0.3


def padded_2(block, sides, width):
    for axis, dim in sides:
        count = lax.axis_size(axis)
        forward = [(i, i + 1) for i in range(count - 1)]
        backward = [(target, source) for source, target in forward]
        low = lax.ppermute(
            lax.slice_in_dim(block, block.shape[dim] - width, None, axis=dim), axis, forward
        )
        high = lax.ppermute(lax.slice_in_dim(block, 0, width, axis=dim), axis, backward)
        block = jnp.concatenate([low, block, high], axis=dim)
    return block


def activate(value):
    return SLOPE * value + (1.0 - SLOPE) * value * jax.nn.sigmoid(value)


def activate_slope(value):
    sig = jax.nn.sigmoid(value)
    return SLOPE + (1.0 - SLOPE) * (sig + value * sig * (1.0 - sig))


def conv_depth(padded, kernel):
    return lax.conv_general_dilated(
        padded[None],
        kernel,
        (1, 1, 1),
        [(0, 0), (1, 1), (1, 1)],
        dimension_numbers=("NDHWC", "DHWIO", "NDHWC"),
        preferred_element_type=jnp.float32,
    )[0]


def pool_cells(values):
    dd, hh, ww, cc = values.shape
    return values.reshape(dd // 2, 2, hh // 2, 2, ww // 2, 2, cc).mean(axis=(1, 3, 5))


def expand(values):
    return jnp.repeat(jnp.repeat(jnp.repeat(values, 2, 0), 2, 1), 2, 2)


def kernel_grad(padded, cotangent):
    dd, hh, ww, _ = cotangent.shape
    tap_list = []
    for depth_off in range(3):
        for row_off in range(3):
            for col_off in range(3):
                window = padded[
                    depth_off : depth_off + dd, row_off : row_off + hh, col_off : col_off + ww
                ]
                tap_list.append(
                    jnp.einsum(
                        "dhwi,dhwo->io", window, cotangent, preferred_element_type=jnp.float32
                    )
                )
    return jnp.stack(tap_list).reshape(3, 3, 3, padded.shape[-1], cotangent.shape[-1])


def pad_sides(values):
    return jnp.pad(values, ((0, 0), (1, 1), (1, 1), (0, 0)))


def pad_depth(values):
    return jnp.pad(values, ((1, 1), (0, 0), (0, 0), (0, 0)))


def pad_cells(values):
    return jnp.pad(values, ((1, 1), (1, 1), (1, 1), (0, 0)))


def on_device(volume, first_kernel, mid_kernel, deep_kernel, deep_cotangent):
    slab_depth = volume.shape[1]
    side_cells = volume.shape[2]
    in_channels = volume.shape[3] // side_cells
    space_count = lax.axis_size("space")
    space_index = lax.axis_index("space")
    input_field = volume[0].reshape(slab_depth, side_cells, side_cells, in_channels)
    padded = padded_2(input_field, (("space", 0),), 1)
    own_hidden = activate(conv_depth(padded, first_kernel)).astype(jnp.bfloat16)
    hidden = padded_2(own_hidden, (("space", 0),), 1)
    pre_mid = conv_depth(hidden, mid_kernel)
    pooled = pool_cells(activate(pre_mid)).astype(jnp.bfloat16)
    cotangent = deep_cotangent[0].astype(jnp.float32)
    columns = lax.all_to_all(pooled, "space", split_axis=3, concat_axis=0, tiled=True)
    chan_width = columns.shape[3]
    chan_start = space_index * chan_width
    kernel_part = lax.dynamic_slice_in_dim(deep_kernel, chan_start, chan_width, 3)
    partial_value = conv_depth(pad_depth(columns), kernel_part)
    pre_deep = lax.psum_scatter(partial_value, "space", scatter_dimension=0, tiled=True)
    grad_pre = (cotangent * activate_slope(pre_deep)).astype(jnp.bfloat16)
    all_cotangent = lax.all_gather(grad_pre, "space", axis=0, tiled=True)
    deep_grad = kernel_grad(pad_cells(columns), all_cotangent)
    flipped_part = jnp.swapaxes(kernel_part[::-1, ::-1, ::-1], 3, 4)
    back_grad = conv_depth(pad_depth(all_cotangent), flipped_part).astype(jnp.bfloat16)
    pooled_grad = lax.all_to_all(back_grad, "space", split_axis=0, concat_axis=3, tiled=True)
    deep_grad = lax.psum(deep_grad.astype(jnp.bfloat16), "dp").astype(jnp.float32)
    grad_mid = (expand(pooled_grad.astype(jnp.float32)) * 0.125 * activate_slope(pre_mid)).astype(
        jnp.bfloat16
    )
    mid_grad = lax.psum(kernel_grad(pad_sides(hidden), grad_mid), ("dp", "space"))
    device_total = lax.axis_size("dp") * space_count
    cell_count = slab_depth * side_cells * side_cells
    deep_scale = math.sqrt(device_total * cell_count // 8)
    mid_scale = math.sqrt(device_total * cell_count)
    deep_output = activate(pre_deep).astype(jnp.bfloat16)[None]
    return (deep_output, deep_grad / deep_scale, mid_grad / mid_scale)


def solution(mesh):
    in_specs = (P("dp", "space", None, None), P(), P(), P(), P("dp", "space", None, None, None))
    out_specs = (P("dp", "space", None, None, None), P(None, None, None, "space", None), P())
    return jax.shard_map(
        on_device, mesh=mesh, in_specs=in_specs, out_specs=out_specs, check_vma=False
    )
```

profile of v0, /device:TPU:1, one launch (start us, length us, event | category | flops | bytes accessed | tf_op | source)
XLA Modules:
  0.0 628.2 jit_solution(16983838333227108347)
XLA Ops:
  8.2 4.0 collective-permute-start
  12.3 1.3 collective-permute-start.1
  13.6 3.4 collective-permute-done.1
  18.2 7.4 %add_convert_fusion = (bf16[4,32,8,5,64]{4,2,3,1,0:T(8,128)(2,1)}, f32[4,32,8,5,64]{4,2,3,1,0:T(8,128)S(1)}, f32[4,32,8,5,64]{4,2,3,1,0:T(8,128)S(1)}, f32[4,32,8,5,64]{4,2,3,1,0:T(8,128)S(1)}) fusion(pred[8,5]{0,1:T(8,128)(4,1)S(1)} %copy-done.21, bf16[3,3,3,4,64]{4,3,2,1,0:T(4,128)(2,1)S(1)} %copy-done.20, bf16[6,32,1,7,2,4]{3,5,4,1,0,2:T(4,128)(2,1)S(1)} %slice.257, ...), kind=kOutput, calls=%fused_computation.31 | convolution fusion | flops 72511488 | bytes 4684328 | tf_op jit(solution)/shard_map/conv_general_dilated | solution.py:33
  27.5 4.8 fusion.30
  32.4 4.3 collective-permute-start.2
  36.7 1.3 collective-permute-start.3
  38.0 2.0 collective-permute-done.2
  40.0 7.1 %collective-permute-done.3 = bf16[1,32,32,64]{3,2,1,0:T(8,128)(2,1)S(1)} collective-permute-done((bf16[1,32,32,64]{3,2,1,0:T(8,128)(2,1)S(1)}, bf16[1,32,32,64]{3,2,1,0:T(8,128)(2,1)S(1)}, u32[]{:S(2)}, u32[]{:S(2)}) %collective-permute-start.3) | collective-permute-done | bytes 131104 | tf_op jit(solution)/shard_map/ppermute | solution.py:18
  47.0 1.5 pad_maximum_fusion
  50.6 6.6 %broadcast_multiply_fusion.1 = (f32[4,32,8,5,128]{4,2,3,1,0:T(8,128)S(1)}, f32[4,32,8,5,128]{4,2,3,1,0:T(8,128)S(1)}, f32[4,32,8,5,128]{4,2,3,1,0:T(8,128)S(1)}, f32[4,32,8,5,128]{4,2,3,1,0:T(8,128)}) fusion(bf16[3,3,3,64,128]{4,3,2,1,0:T(8,128)(2,1)S(1)} %copy-done.19, bf16[6,32,1,7,2,64]{5,3,4,1,0,2:T(8,128)(2,1)S(1)} %slice.263, ...), kind=kOutput, calls=%fused_computation.97 | convolution fusion | flops 2225799168 | bytes 12255272 | tf_op jit(solution)/shard_map/conv_general_dilated | solution.py:33
  58.6 2.1 fusion.28
  60.7 2.9 reduce_sum.9
  63.6 1.7 copy.210
  65.3 1.7 reshape.223
  67.0 5.2 all-to-all-start
  72.3 5.5 all-to-all-done
  77.8 1.7 reshape.224
  79.5 1.6 copy.212
  81.1 1.3 pad_bitcast_fusion.1
  82.5 4.0 copy.321
  86.4 2.8 pad.24.clone
  89.3 5.7 copy.215
  94.9 1.7 slice.267
  96.8 4.5 broadcast_select_fusion
  101.3 2.0 copy.216
  103.3 2.4 slice_bitcast_fusion
  106.2 93.6 %reduce-scatter.2.cloned.1.call-done = f32[2,16,16,256]{3,1,2,0:T(8,128)} async-done(((f32[16,16,16,256]{3,1,2,0:T(8,128)}), f32[2,16,16,256]{3,1,2,0:T(8,128)}) %reduce-scatter.2.cloned.1.call-update) | async-done | bytes 524304 | tf_op jit(solution)/shard_map/reduce_scatter | solution.py:99
  199.9 1.4 fusion.233
  202.1 1.7 copy.240
  205.3 1.5 copy-done.3
  206.8 1.5 slice.271
  208.3 46.0 %all-gather.2.cloned.1.call-done = bf16[16,16,16,256]{3,2,1,0:T(8,128)(2,1)} async-done(((bf16[2,16,16,256]{3,2,1,0:T(8,128)(2,1)}), bf16[16,16,16,256]{3,2,1,0:T(8,128)(2,1)}) %all-gather.2.cloned.1.call-update) | async-done | bytes 2097168 | tf_op jit(solution)/shard_map/all_gather | solution.py:101
  254.3 2.5 copy.219
  257.4 1.6 copy.221
  259.6 22.7 %select_convert_fusion = bf16[16,16,8,3,16]{4,2,3,1,0:T(8,128)(2,1)S(1)} fusion(pred[8,3]{0,1:T(4,128)(4,1)S(1)} %copy-done.22, bf16[18,16,1,7,2,256]{5,3,4,1,0,2:T(8,128)(2,1)S(1)} %slice.269, bf16[18,16,1,8,3,256]{5,3,4,1,0,2:T(8,128)(2,1)S(1)} %copy.221, bf16[3,3,3,128,256]{4,3,2,1,0:T(8,128)(2,1)S(1)} %copy-done, s32[]{:T(128)S(6)} %select_n.3), kind=kOutput, calls=%fused_computation.13 | convolution fusion | flops 1320222720 | bytes 6316548 | tf_op jit(solution)/shard_map/conv_general_dilated | solution.py:33
  283.9 3.1 reshape.225
  287.0 3.4 all-to-all-start.1
  290.6 3.0 fusion.179
  293.5 2.9 fusion.177
  296.5 1.4 fusion.175
  297.9 1.4 fusion.173
  300.5 1.4 fusion.169
  301.9 1.4 fusion.167
  304.5 1.4 fusion.163
  305.9 1.4 fusion.161
  308.5 1.4 fusion.157
  309.9 1.4 fusion.155
  312.5 1.4 fusion.151
  314.0 1.6 fusion.149
  316.8 1.4 fusion.145
  318.2 1.4 fusion.143
  320.8 1.4 fusion.139
  322.2 1.4 fusion.137
  324.9 1.4 fusion.133
  326.3 1.4 fusion.131
  329.0 1.4 fusion.127
  332.1 2.6 copy.314
  334.7 2.6 reshape.222
  340.8 1.5 copy-done.4
  365.0 101.8 %all-reduce.7.cloned.1.call-done = bf16[3,3,3,16,256]{4,3,2,1,0:T(8,128)(2,1)} async-done(((bf16[3,3,3,16,256]{4,3,2,1,0:T(8,128)(2,1)}), bf16[3,3,3,16,256]{4,3,2,1,0:T(8,128)(2,1)}) %all-reduce.7.cloned.1.call-update) | async-done | bytes 221200 | tf_op jit(solution)/shard_map/psum | solution.py:106
  466.9 1.7 convert_multiply_fusion.2
  468.6 150.7 %all-reduce.9.cloned.1.call-done = f32[3,3,3,64,128]{4,3,2,1,0:T(8,128)} async-done(((f32[3,3,3,64,128]{4,3,2,1,0:T(8,128)}), f32[3,3,3,64,128]{4,3,2,1,0:T(8,128)}) %all-reduce.9.cloned.1.call-update) | async-done | bytes 884752 | tf_op jit(solution)/shard_map/psum | solution.py:110
  619.3 2.2 broadcast_multiply_fusion.2
  (127 shorter events, 50.9 us)
Async XLA Ops:
  7.2 89.5 %copy-start = (bf16[3,3,3,128,256]{4,3,2,1,0:T(8,128)(2,1)S(1)}, bf16[3,3,3,128,256]{4,3,2,1,0:T(8,128)(2,1)}, u32[]{:S(2)}) copy-start(bf16[3,3,3,128,256]{4,3,2,1,0:T(8,128)(2,1)} %param.8) | copy-start | bytes 5308420
  7.2 11.0 %copy-start.21 = (pred[8,5]{0,1:T(8,128)(4,1)S(1)}, pred[8,5]{0,1:T(8,128)(4,1)}, u32[]{:S(2)}) copy-start(pred[8,5]{0,1:T(8,128)(4,1)} %constant.63) | copy-start | bytes 124
  7.2 11.0 %copy-start.20 = (bf16[3,3,3,4,64]{4,3,2,1,0:T(4,128)(2,1)S(1)}, bf16[3,3,3,4,64]{4,3,2,1,0:T(4,128)(2,1)}, u32[]{:S(2)}) copy-start(bf16[3,3,3,4,64]{4,3,2,1,0:T(4,128)(2,1)} %param.6) | copy-start | bytes 41476
  8.2 5.3 collective-permute-start
  12.3 4.7 collective-permute-start.1
  32.3 16.2 %copy-start.6 = (bf16[4,32,1,32,64]{4,3,1,2,0:T(8,128)(2,1)}, bf16[4,32,1,32,64]{4,3,1,2,0:T(8,128)(2,1)S(1)}, u32[]{:S(2)}) copy-start(bf16[4,32,1,32,64]{4,3,1,2,0:T(8,128)(2,1)S(1)} %fusion.30) | copy-start | bytes 1572868
  32.4 7.6 %collective-permute-start.2 = (bf16[1,32,32,64]{3,2,1,0:T(8,128)(2,1)S(1)}, bf16[1,32,32,64]{3,2,1,0:T(8,128)(2,1)S(1)}, u32[]{:S(2)}, u32[]{:S(2)}) collective-permute-start(bf16[1,32,32,64]{3,2,1,0:T(8,128)(2,1)S(1)} %get-tuple-element.18), channel_id=1, source_target_pairs={{0,1},{1,2},{2,3},{3,4},{4,5},{5,6},{6,7},{8,9},{9,10},{10,11},{11... | collective-permute-start | bytes 393224 | tf_op jit(solution)/shard_map/ppermute | solution.py:15
  36.7 10.3 %collective-permute-start.3 = (bf16[1,32,32,64]{3,2,1,0:T(8,128)(2,1)S(1)}, bf16[1,32,32,64]{3,2,1,0:T(8,128)(2,1)S(1)}, u32[]{:S(2)}, u32[]{:S(2)}) collective-permute-start(bf16[1,32,32,64]{3,2,1,0:T(8,128)(2,1)S(1)} %get-tuple-element.19), channel_id=1, source_target_pairs={{1,0},{2,1},{3,2},{4,3},{5,4},{6,5},{7,6},{9,8},{10,9},{11,10},{12... | collective-permute-start | bytes 393224 | tf_op jit(solution)/shard_map/ppermute | solution.py:18
  40.0 8.6 %copy-start.16 = (bf16[1,32,32,64]{3,2,1,0:T(8,128)(2,1)}, bf16[1,32,32,64]{3,2,1,0:T(8,128)(2,1)S(1)}, u32[]{:S(2)}) copy-start(bf16[1,32,32,64]{3,2,1,0:T(8,128)(2,1)S(1)} %collective-permute-done.2) | copy-start | bytes 393220
  47.0 1.5 copy-start.14
  49.6 1.0 copy-start.19
  67.0 10.8 %all-to-all-start = ((bf16[8,2,4096]{2,1,0:T(2,128)(2,1)}), bf16[8,2,4096]{2,1,0:T(2,128)(2,1)S(1)}, u32[]{:S(2)}, u32[]{:S(2)}) async-start(bf16[8,2,4096]{2,1,0:T(2,128)(2,1)} %reshape.223), calls=%async_computation | async-start | bytes 262144 | tf_op jit(solution)/shard_map/all_to_all | solution.py:94
  72.3 127.6 %reduce-scatter.2.cloned.1.call-start = ((), (), s32[]{:S(2)}) async-start(), calls=%async_computation.3 | async-start | bytes 4718592 | tf_op jit(solution)/shard_map/reduce_scatter | solution.py:99
  89.3 7.4 %copy-start.22 = (pred[8,3]{0,1:T(4,128)(4,1)S(1)}, pred[8,3]{0,1:T(4,128)(4,1)}, u32[]{:S(2)}) copy-start(pred[8,3]{0,1:T(4,128)(4,1)} %constant.62) | copy-start | bytes 76
  94.9 1.8 copy-start.8
  105.7 94.1 %copy-start.13 = (bf16[1,2,16,16,256]{4,3,2,1,0:T(8,128)(2,1)S(1)}, bf16[1,2,16,16,256]{4,3,2,1,0:T(8,128)(2,1)}, u32[]{:S(2)}) copy-start(bf16[1,2,16,16,256]{4,3,2,1,0:T(8,128)(2,1)} %param.9) | copy-start | bytes 786436
  105.8 148.5 %all-gather.2.cloned.1.call-start = ((), (), s32[]{:S(2)}) async-start(), calls=%async_computation.4 | async-start | bytes 2359296 | tf_op jit(solution)/shard_map/all_gather | solution.py:101
  202.0 2.8 copy-start.9
  205.3 1.5 copy-start.3
  287.0 44.2 %all-to-all-start.1 = ((bf16[8,2,4096]{2,1,0:T(2,128)(2,1)}), bf16[8,2,4096]{2,1,0:T(2,128)(2,1)S(1)}, u32[]{:S(2)}, u32[]{:S(2)}) async-start(bf16[8,2,4096]{2,1,0:T(2,128)(2,1)} %reshape.225), calls=%async_computation.2 | async-start | bytes 262144 | tf_op jit(solution)/shard_map/all_to_all | solution.py:105
  290.4 176.5 %all-reduce.7.cloned.1.call-start = ((), (), s32[]{:S(2)}) async-start(), calls=%async_computation.5 | async-start | bytes 442368 | tf_op jit(solution)/shard_map/psum | solution.py:106
  293.5 2.9 copy-start.2
  330.4 0.7 copy-start.18
  331.1 288.2 %all-reduce.9.cloned.1.call-start = ((), (), s32[]{:S(2)}) async-start(), calls=%async_computation.6 | async-start | bytes 1769472 | tf_op jit(solution)/shard_map/psum | solution.py:110
  337.2 1.6 copy-start.5
  340.6 1.8 copy-start.4
  342.3 1.4 copy-start.10
  345.7 1.2 copy-start.7
  345.7 1.3 copy-start.17
  352.4 1.2 copy-start.11
  359.0 1.0 copy-start.15
  362.6 258.9 %copy-start.1 = (bf16[3,3,3,128,256]{4,3,2,1,0:T(8,128)(2,1)S(1)}, bf16[3,3,3,128,256]{4,3,2,1,0:T(8,128)(2,1)}, u32[]{:S(2)}) copy-start(bf16[3,3,3,128,256]{4,3,2,1,0:T(8,128)(2,1)} %param.8) | copy-start | bytes 5308420
  363.3 0.9 copy-start.12
Sparse Core Ops, SparseCore 0:
  105.9 93.9 reduce-scatter.1
  202.2 52.0 all-gather.1
  331.2 135.5 all-reduce.6
  472.8 146.4 all-reduce.8
where the time goes:
time: 638 us; the launch traced here: 628 us
  waiting for transfers between devices  410 us (64%)
  matrix products  99 us (16%)
  local copies, waits for them, and re-layouts  65.3 us (10%)
  starting transfers between devices  20.2 us (3%)
  other arithmetic  18.8 us (3%)
  between operations  14.7 us (2%)
    psum x1, waiting for transfers between devices, on_device(): lax.psum(kernel_grad(pad_sides(hidden), grad_mid), ('dp', 'space'))  151 us
    psum x1, waiting for transfers between devices, on_device(): lax.psum(deep_grad.astype(jnp.bfloat16), 'dp').astype(jnp.float32)  102 us
    reduce_scatter x1, waiting for transfers between devices, on_device(): lax.psum_scatter(partial_value, 'space', scatter_dimension=0, tiled=True)  93.6 us
    dot_general x54, matrix products, kernel_grad(): jnp.einsum('dhwi,dhwo->io', window, cotangent, preferred_element_type=jnp...  57.9 us
    all_gather x1, waiting for transfers between devices, on_device(): all_cotangent = lax.all_gather(grad_pre, 'space', axis=0, tiled=True)  46 us
    conv_general_dilated x4, matrix products, conv_depth(): lax.conv_general_dilated(padded[None], kernel, (1, 1, 1), [(0, 0), (1, 1)...  41.1 us
    unnamed x55, local copies, waits for them, and re-layouts  22.3 us
    conv_general_dilated x11, local copies, waits for them, and re-layouts, conv_depth(): lax.conv_general_dilated(padded[None], kernel, (1, 1, 1), [(0, 0), (1, 1)...  15.4 us
  transfers between devices with their start and end apart: 10, of which 8 were waited for; matrix products, arithmetic and copies ran while one was open for 12% of the time, Pallas kernels for 0%

commit v1 on v0

--- a/solution.py
+++ b/solution.py
@@ -3,8 +3,13 @@
 import jax.numpy as jnp
 from jax import lax
 from jax.sharding import PartitionSpec as P
+from jax.lax import all_gather
 
 SLOPE = 0.3
+
+
+def sides_show(panel):
+    return jnp.sum(all_gather(panel, "dp"), 0)
 
 
 def padded_2(block, sides, width):
@@ -103,7 +108,7 @@
     flipped_part = jnp.swapaxes(kernel_part[::-1, ::-1, ::-1], 3, 4)
     back_grad = conv_depth(pad_depth(all_cotangent), flipped_part).astype(jnp.bfloat16)
     pooled_grad = lax.all_to_all(back_grad, "space", split_axis=0, concat_axis=3, tiled=True)
-    deep_grad = lax.psum(deep_grad.astype(jnp.bfloat16), "dp").astype(jnp.float32)
+    deep_grad = sides_show(deep_grad.astype(jnp.bfloat16)).astype(jnp.float32)
     grad_mid = (expand(pooled_grad.astype(jnp.float32)) * 0.125 * activate_slope(pre_mid)).astype(
         jnp.bfloat16
     )

time: 638 us -> 594 us (0.931)
  waiting for transfers between devices: 410 us -> 352 us
  other arithmetic: 18.8 us -> 29.5 us
    psum x1 -> x0, waiting for transfers between devices: 102 us -> none  [on_device(): lax.psum(deep_grad.astype(jnp.bfloat16), 'dp').astype(jnp.float32)]
    all_gather x0 -> x1, waiting for transfers between devices: none -> 53.5 us  [sides_show(): return jnp.sum(all_gather(panel, 'dp'), 0)]
    psum x1, waiting for transfers between devices: 151 us -> 141 us  [on_device(): lax.psum(kernel_grad(pad_sides(hidden), grad_mid), ('dp', 'space'))]
    convert_element_type x1, other arithmetic: 4.8 us -> 13.7 us  [on_device(): own_hidden = activate(conv_depth(padded, first_kernel)).astype(jnp.bfloat16)]
  transfers between devices with their start and end apart: 10 -> 10, of which waited for: 8 -> 8; matrix products, arithmetic and copies ran while one was open for 12% -> 9% of each run, Pallas kernels for 0% -> 0%
where the time goes in v1:
time: 594 us; the launch traced here: 584 us
  waiting for transfers between devices  352 us (59%)
  matrix products  102 us (17%)
  local copies, waits for them, and re-layouts  65.3 us (11%)
  other arithmetic  29.5 us (5%)
  starting transfers between devices  20 us (3%)
  between operations  14.7 us (2%)
    psum x1, waiting for transfers between devices, on_device(): lax.psum(kernel_grad(pad_sides(hidden), grad_mid), ('dp', 'space'))  141 us
    reduce_scatter x1, waiting for transfers between devices, on_device(): lax.psum_scatter(partial_value, 'space', scatter_dimension=0, tiled=True)  93.9 us
    dot_general x54, matrix products, kernel_grad(): jnp.einsum('dhwi,dhwo->io', window, cotangent, preferred_element_type=jnp...  61.3 us
    all_gather x1, waiting for transfers between devices, sides_show(): return jnp.sum(all_gather(panel, 'dp'), 0)  53.5 us
    all_gather x1, waiting for transfers between devices, on_device(): all_cotangent = lax.all_gather(grad_pre, 'space', axis=0, tiled=True)  46 us
    conv_general_dilated x4, matrix products, conv_depth(): lax.conv_general_dilated(padded[None], kernel, (1, 1, 1), [(0, 0), (1, 1)...  41.1 us
    unnamed x55, local copies, waits for them, and re-layouts  22.3 us
    conv_general_dilated x11, local copies, waits for them, and re-layouts, conv_depth(): lax.conv_general_dilated(padded[None], kernel, (1, 1, 1), [(0, 0), (1, 1)...  15.4 us
  transfers between devices with their start and end apart: 10, of which 8 were waited for; matrix products, arithmetic and copies ran while one was open for 9% of the time, Pallas kernels for 0%

profile of v1, /device:TPU:1, one launch (start us, length us, event | category | flops | bytes accessed | tf_op | source)
XLA Modules:
  0.0 584.3 jit_solution(4557847056751175654)
XLA Ops:
  8.2 4.0 collective-permute-start
  12.3 1.3 collective-permute-start.1
  13.6 3.4 collective-permute-done.1
  18.2 7.4 %add_convert_fusion = (bf16[4,32,8,5,64]{4,2,3,1,0:T(8,128)(2,1)}, f32[4,32,8,5,64]{4,2,3,1,0:T(8,128)S(1)}, f32[4,32,8,5,64]{4,2,3,1,0:T(8,128)S(1)}, f32[4,32,8,5,64]{4,2,3,1,0:T(8,128)S(1)}) fusion(pred[8,5]{0,1:T(8,128)(4,1)S(1)} %copy-done.21, bf16[3,3,3,4,64]{4,3,2,1,0:T(4,128)(2,1)S(1)} %copy-done.20, bf16[6,32,1,7,2,4]{3,5,4,1,0,2:T(4,128)(2,1)S(1)} %slice.257, ...), kind=kOutput, calls=%fused_computation.31 | convolution fusion | flops 72511488 | bytes 4684328 | tf_op jit(solution)/shard_map/conv_general_dilated | solution.py:38
  27.5 13.7 %fusion.30 = bf16[4,32,1,32,64]{4,3,1,2,0:T(8,128)(2,1)S(1)} fusion(f32[4,32,1,32,64]{4,1,3,0,2:T(8,128)S(1)} %slice.260, f32[4,32,1,32,64]{4,1,3,0,2:T(8,128)S(1)} %slice.259, f32[4,32,1,32,64]{4,1,3,0,2:T(8,128)S(1)} %slice.258), kind=kLoop, calls=%fused_computation.64 | loop fusion | flops 786432 | bytes 3670016 | tf_op jit(solution)/shard_map/convert_element_type | solution.py:94
  41.3 4.3 collective-permute-start.2
  46.9 2.0 collective-permute-done.2
  48.9 7.1 %collective-permute-done.3 = bf16[1,32,32,64]{3,2,1,0:T(8,128)(2,1)S(1)} collective-permute-done((bf16[1,32,32,64]{3,2,1,0:T(8,128)(2,1)S(1)}, bf16[1,32,32,64]{3,2,1,0:T(8,128)(2,1)S(1)}, u32[]{:S(2)}, u32[]{:S(2)}) %collective-permute-start.3) | collective-permute-done | bytes 131104 | tf_op jit(solution)/shard_map/ppermute | solution.py:23
  55.9 1.5 pad_maximum_fusion
  59.5 6.6 %broadcast_multiply_fusion.1 = (f32[4,32,8,5,128]{4,2,3,1,0:T(8,128)S(1)}, f32[4,32,8,5,128]{4,2,3,1,0:T(8,128)S(1)}, f32[4,32,8,5,128]{4,2,3,1,0:T(8,128)S(1)}, f32[4,32,8,5,128]{4,2,3,1,0:T(8,128)}) fusion(bf16[3,3,3,64,128]{4,3,2,1,0:T(8,128)(2,1)S(1)} %copy-done.19, bf16[6,32,1,7,2,64]{5,3,4,1,0,2:T(8,128)(2,1)S(1)} %slice.263, ...), kind=kOutput, calls=%fused_computation.97 | convolution fusion | flops 2225799168 | bytes 12255272 | tf_op jit(solution)/shard_map/conv_general_dilated | solution.py:38
  67.5 2.1 fusion.28
  69.6 2.9 reduce_sum.21
  72.6 1.9 copy.210
  74.4 1.7 reshape.233
  76.2 5.2 all-to-all-start
  81.4 5.5 all-to-all-done
  86.9 1.7 reshape.234
  88.7 1.6 copy.212
  90.3 1.3 pad_bitcast_fusion.1
  91.6 4.0 copy.321
  95.6 2.8 pad.24.clone
  98.4 5.7 copy.215
  104.1 1.7 slice.267
  105.9 4.5 broadcast_select_fusion
  110.5 2.0 copy.216
  112.4 2.4 slice_bitcast_fusion
  115.1 93.9 %reduce-scatter.2.cloned.1.call-done = f32[2,16,16,256]{3,1,2,0:T(8,128)} async-done(((f32[16,16,16,256]{3,1,2,0:T(8,128)}), f32[2,16,16,256]{3,1,2,0:T(8,128)}) %reduce-scatter.2.cloned.1.call-update) | async-done | bytes 524304 | tf_op jit(solution)/shard_map/reduce_scatter | solution.py:104
  209.0 1.4 fusion.233
  211.2 1.7 copy.240
  214.5 1.5 copy-done.3
  216.0 1.5 slice.271
  217.5 46.0 %all-gather.3.cloned.1.call-done = bf16[16,16,16,256]{3,2,1,0:T(8,128)(2,1)} async-done(((bf16[2,16,16,256]{3,2,1,0:T(8,128)(2,1)}), bf16[16,16,16,256]{3,2,1,0:T(8,128)(2,1)}) %all-gather.3.cloned.1.call-update) | async-done | bytes 2097168 | tf_op jit(solution)/shard_map/all_gather | solution.py:106
  263.4 2.5 copy.219
  266.5 1.6 copy.221
  268.7 22.7 %select_convert_fusion = bf16[16,16,8,3,16]{4,2,3,1,0:T(8,128)(2,1)S(1)} fusion(pred[8,3]{0,1:T(4,128)(4,1)S(1)} %copy-done.22, bf16[18,16,1,7,2,256]{5,3,4,1,0,2:T(8,128)(2,1)S(1)} %slice.269, bf16[18,16,1,8,3,256]{5,3,4,1,0,2:T(8,128)(2,1)S(1)} %copy.221, bf16[3,3,3,128,256]{4,3,2,1,0:T(8,128)(2,1)S(1)} %copy-done, s32[]{:T(128)S(6)} %select_n.3), kind=kOutput, calls=%fused_computation.13 | convolution fusion | flops 1320222720 | bytes 6316548 | tf_op jit(solution)/shard_map/conv_general_dilated | solution.py:38
  293.0 3.1 reshape.235
  296.1 3.4 all-to-all-start.1
  299.8 3.0 fusion.179
  302.7 2.9 fusion.177
  305.7 1.4 fusion.175
  307.0 1.4 fusion.173
  309.7 1.4 fusion.169
  311.1 1.4 fusion.167
  313.7 1.4 fusion.163
  315.1 1.4 fusion.161
  317.7 1.4 fusion.157
  319.1 1.4 fusion.155
  321.7 1.4 fusion.151
  323.2 1.8 fusion.149
  326.2 1.4 fusion.145
  327.6 1.4 fusion.143
  330.2 1.4 fusion.139
  331.6 1.4 fusion.137
  334.3 1.4 fusion.133
  335.7 1.4 fusion.131
  338.0 2.6 copy.314
  340.6 2.3 reshape.232
  346.6 1.5 copy-done.4
  370.1 2.8 fusion.129
  372.9 3.0 fusion.127
  377.4 140.9 %all-reduce.6.cloned.1.call-done = f32[3,3,3,64,128]{4,3,2,1,0:T(8,128)} async-done(((f32[3,3,3,64,128]{4,3,2,1,0:T(8,128)}), f32[3,3,3,64,128]{4,3,2,1,0:T(8,128)}) %all-reduce.6.cloned.1.call-update) | async-done | bytes 884752 | tf_op jit(solution)/shard_map/psum | solution.py:115
  518.3 2.3 broadcast_multiply_fusion.2
  520.6 53.5 %all-gather.5.cloned.1.call-done = bf16[16,3,3,3,16,256]{5,4,3,2,1,0:T(8,128)(2,1)} async-done(((bf16[1,3,3,3,16,256]{5,4,3,2,1,0:T(8,128)(2,1)}), bf16[16,3,3,3,16,256]{5,4,3,2,1,0:T(8,128)(2,1)}) %all-gather.5.cloned.1.call-update) | async-done | bytes 3538960 | tf_op jit(solution)/shard_map/all_gather | solution.py:12
  574.1 2.6 reduce_sum.22
  (128 shorter events, 51.7 us)
Async XLA Ops:
  7.2 98.6 %copy-start = (bf16[3,3,3,128,256]{4,3,2,1,0:T(8,128)(2,1)S(1)}, bf16[3,3,3,128,256]{4,3,2,1,0:T(8,128)(2,1)}, u32[]{:S(2)}) copy-start(bf16[3,3,3,128,256]{4,3,2,1,0:T(8,128)(2,1)} %param.8) | copy-start | bytes 5308420
  7.2 11.0 %copy-start.21 = (pred[8,5]{0,1:T(8,128)(4,1)S(1)}, pred[8,5]{0,1:T(8,128)(4,1)}, u32[]{:S(2)}) copy-start(pred[8,5]{0,1:T(8,128)(4,1)} %constant.64) | copy-start | bytes 124
  7.2 11.0 %copy-start.20 = (bf16[3,3,3,4,64]{4,3,2,1,0:T(4,128)(2,1)S(1)}, bf16[3,3,3,4,64]{4,3,2,1,0:T(4,128)(2,1)}, u32[]{:S(2)}) copy-start(bf16[3,3,3,4,64]{4,3,2,1,0:T(4,128)(2,1)} %param.6) | copy-start | bytes 41476
  8.2 5.3 collective-permute-start
  12.3 4.7 collective-permute-start.1
  41.3 16.2 %copy-start.6 = (bf16[4,32,1,32,64]{4,3,1,2,0:T(8,128)(2,1)}, bf16[4,32,1,32,64]{4,3,1,2,0:T(8,128)(2,1)S(1)}, u32[]{:S(2)}) copy-start(bf16[4,32,1,32,64]{4,3,1,2,0:T(8,128)(2,1)S(1)} %fusion.30) | copy-start | bytes 1572868
  41.3 7.6 %collective-permute-start.2 = (bf16[1,32,32,64]{3,2,1,0:T(8,128)(2,1)S(1)}, bf16[1,32,32,64]{3,2,1,0:T(8,128)(2,1)S(1)}, u32[]{:S(2)}, u32[]{:S(2)}) collective-permute-start(bf16[1,32,32,64]{3,2,1,0:T(8,128)(2,1)S(1)} %get-tuple-element.18), channel_id=1, source_target_pairs={{0,1},{1,2},{2,3},{3,4},{4,5},{5,6},{6,7},{8,9},{9,10},{10,11},{11... | collective-permute-start | bytes 393224 | tf_op jit(solution)/shard_map/ppermute | solution.py:20
  45.6 10.3 %collective-permute-start.3 = (bf16[1,32,32,64]{3,2,1,0:T(8,128)(2,1)S(1)}, bf16[1,32,32,64]{3,2,1,0:T(8,128)(2,1)S(1)}, u32[]{:S(2)}, u32[]{:S(2)}) collective-permute-start(bf16[1,32,32,64]{3,2,1,0:T(8,128)(2,1)S(1)} %get-tuple-element.19), channel_id=1, source_target_pairs={{1,0},{2,1},{3,2},{4,3},{5,4},{6,5},{7,6},{9,8},{10,9},{11,10},{12... | collective-permute-start | bytes 393224 | tf_op jit(solution)/shard_map/ppermute | solution.py:23
  48.9 8.6 %copy-start.16 = (bf16[1,32,32,64]{3,2,1,0:T(8,128)(2,1)}, bf16[1,32,32,64]{3,2,1,0:T(8,128)(2,1)S(1)}, u32[]{:S(2)}) copy-start(bf16[1,32,32,64]{3,2,1,0:T(8,128)(2,1)S(1)} %collective-permute-done.2) | copy-start | bytes 393220
  55.9 1.5 copy-start.14
  58.5 1.0 copy-start.19
  76.2 10.8 %all-to-all-start = ((bf16[8,2,4096]{2,1,0:T(2,128)(2,1)}), bf16[8,2,4096]{2,1,0:T(2,128)(2,1)S(1)}, u32[]{:S(2)}, u32[]{:S(2)}) async-start(bf16[8,2,4096]{2,1,0:T(2,128)(2,1)} %reshape.233), calls=%async_computation | async-start | bytes 262144 | tf_op jit(solution)/shard_map/all_to_all | solution.py:99
  81.4 127.6 %reduce-scatter.2.cloned.1.call-start = ((), (), s32[]{:S(2)}) async-start(), calls=%async_computation.3 | async-start | bytes 4718592 | tf_op jit(solution)/shard_map/reduce_scatter | solution.py:104
  98.4 7.4 %copy-start.22 = (pred[8,3]{0,1:T(4,128)(4,1)S(1)}, pred[8,3]{0,1:T(4,128)(4,1)}, u32[]{:S(2)}) copy-start(pred[8,3]{0,1:T(4,128)(4,1)} %constant.63) | copy-start | bytes 76
  104.1 1.8 copy-start.8
  114.9 94.1 %copy-start.13 = (bf16[1,2,16,16,256]{4,3,2,1,0:T(8,128)(2,1)S(1)}, bf16[1,2,16,16,256]{4,3,2,1,0:T(8,128)(2,1)}, u32[]{:S(2)}) copy-start(bf16[1,2,16,16,256]{4,3,2,1,0:T(8,128)(2,1)} %param.9) | copy-start | bytes 786436
  114.9 148.5 %all-gather.3.cloned.1.call-start = ((), (), s32[]{:S(2)}) async-start(), calls=%async_computation.4 | async-start | bytes 2359296 | tf_op jit(solution)/shard_map/all_gather | solution.py:106
  211.2 2.8 copy-start.9
  214.5 1.5 copy-start.3
  296.1 41.0 %all-to-all-start.1 = ((bf16[8,2,4096]{2,1,0:T(2,128)(2,1)}), bf16[8,2,4096]{2,1,0:T(2,128)(2,1)S(1)}, u32[]{:S(2)}, u32[]{:S(2)}) async-start(bf16[8,2,4096]{2,1,0:T(2,128)(2,1)} %reshape.235), calls=%async_computation.2 | async-start | bytes 262144 | tf_op jit(solution)/shard_map/all_to_all | solution.py:110
  299.5 218.8 %all-reduce.6.cloned.1.call-start = ((), (), s32[]{:S(2)}) async-start(), calls=%async_computation.6 | async-start | bytes 1769472 | tf_op jit(solution)/shard_map/psum | solution.py:115
  302.7 2.9 copy-start.2
  343.0 1.6 copy-start.5
  346.3 1.7 copy-start.4
  348.0 1.4 copy-start.10
  351.5 1.2 copy-start.7
  351.5 1.3 copy-start.17
  358.1 1.2 copy-start.11
  364.8 1.0 copy-start.15
  369.1 0.9 copy-start.12
  370.0 204.1 %all-gather.5.cloned.1.call-start = ((), (), s32[]{:S(2)}) async-start(), calls=%async_computation.5 | async-start | bytes 3760128 | tf_op jit(solution)/shard_map/all_gather | solution.py:12
  375.9 0.7 copy-start.18
  518.3 59.2 %copy-start.1 = (bf16[3,3,3,128,256]{4,3,2,1,0:T(8,128)(2,1)S(1)}, bf16[3,3,3,128,256]{4,3,2,1,0:T(8,128)(2,1)}, u32[]{:S(2)}) copy-start(bf16[3,3,3,128,256]{4,3,2,1,0:T(8,128)(2,1)} %param.8) | copy-start | bytes 5308420
Sparse Core Ops, SparseCore 0:
  115.0 93.9 reduce-scatter.1
  211.3 52.0 all-gather.2
  370.1 148.1 all-reduce.5
  521.5 52.6 all-gather.4
